TPU v7x, 32 devices: a whole 2x2x4 slice. The times are simulated.
32 devices in a mesh: parts: 2 (over y), group: 4 (over x, core), member: 4 (over z), half: 1.
Axes of the slice: x: 2, y: 2, z: 4, core: 2. Of those that a mesh axis runs over, the one named last changes fastest.
Arguments:
- tokens: bfloat16 [2048, 1344], P(('parts', 'group', 'member'), 'half'), parts along dimension 0, may hold values from -120 to 120
- norm_gain: float32 [1344], replicated, may hold values from 0.25 to 1.75
- w_up: bfloat16 [16, 1344, 928], P(('group', 'member'), None, 'half'), may hold values from -0.15625 to 0.15625
- w_down: bfloat16 [16, 928, 1344], P(('group', 'member'), 'half'), may hold values from -0.1875 to 0.1875
- expert_ids: int32 [2048, 6], P(('parts', 'group', 'member')), parts along dimension 0, may hold values from 0 to 15, all different within a row; in each aligned block of 32 rows (0 to 31, 32 to 63, ...) at most 24 rows name the same one
- gates: float32 [2048, 6], P(('parts', 'group', 'member')), parts along dimension 0, may hold values from 0.05 to 0.4
Outputs:
- mixed: bfloat16 [2048, 1344], P(('parts', 'group', 'member'), 'half'), parts along dimension 0
There are 2 independent parts, one for each index of `parts`. A program takes and returns all parts, laid end to end along the dimension named above; an argument that names none is the same for every part. Nothing has to cross between parts.
Inputs may be any that keep to these rules, and one draw needn't show every extreme that they name: `expert_ids`: each token names 6 different experts; in each aligned block of 32 tokens no expert is named by more than 24 tokens, and in some blocks one is named by exactly 24.
All inputs are finite; a program needn't handle non-finite values.
Results may differ from a plain program's by a relative error of at most 0.0073.
Values may be sent and summed in bfloat16 or wider, within the bound.
A program may use at most 64 MiB of HBM per device.

v0:
```python
import jax
import jax.numpy as jnp
from jax import lax
from jax.sharding import PartitionSpec as P

MB_TOK = 32


epsilon = 1e-05


def on_device(tokens, norm_gain, w_up, w_down, expert_ids, gates):
    groups = lax.axis_size("group")
    members = lax.axis_size("member")
    experts = groups * members
    tok_dev, picks = expert_ids.shape
    block_rows = MB_TOK
    capacity = min(block_rows, (2 * picks * block_rows + experts - 1) // experts)
    micro_count = tok_dev // block_rows
    half_width = tokens.shape[1]
    up_local = w_up[0]
    down_local = w_down[0]
    full_rows = lax.all_gather(tokens, "half", axis=1, tiled=True)
    full_float = full_rows.astype(jnp.float32)
    inverse_rms = lax.rsqrt(jnp.mean(full_float * full_float, axis=-1, keepdims=True) + epsilon)
    normed = (full_float * inverse_rms * norm_gain).astype(jnp.bfloat16)
    token_blocks = normed.reshape(micro_count, block_rows, normed.shape[1])
    id_blocks = expert_ids.reshape(micro_count, block_rows, picks)
    gate_blocks = gates.reshape(micro_count, block_rows, picks)

    def one_block(pieces):
        block_tokens, block_ids, weights = pieces
        expert_iota = jnp.arange(experts, dtype=jnp.int32)
        matches = block_ids[:, :, None] == expert_iota[None, None, :]
        picked = jnp.any(matches, axis=1).astype(jnp.int32)
        before = jnp.cumsum(picked, axis=0) - picked
        slot_iota = jnp.arange(capacity, dtype=jnp.int32)
        slot_table = (picked[:, :, None] == 1) & (before[:, :, None] == slot_iota[None, None, :])
        slot_bf = slot_table.astype(jnp.bfloat16).reshape(block_rows, experts * capacity)
        outgoing = lax.dot_general(
            slot_bf, block_tokens, (((0,), (0,)), ((), ())), preferred_element_type=jnp.float32
        )
        outgoing = outgoing.astype(jnp.bfloat16).reshape(experts, capacity, block_tokens.shape[1])
        arrived = lax.all_to_all(
            outgoing, ("group", "member"), split_axis=0, concat_axis=0, tiled=True
        )
        flat_rows = arrived.reshape(experts * capacity, arrived.shape[2])
        up_values = jnp.dot(flat_rows, up_local, preferred_element_type=jnp.float32)
        hidden = jnp.square(jax.nn.relu(up_values)).astype(jnp.bfloat16)
        partial_value = jnp.dot(hidden, down_local, preferred_element_type=jnp.float32).astype(
            jnp.bfloat16
        )
        partial_value = lax.optimization_barrier(partial_value).astype(jnp.float32)
        summed = lax.psum_scatter(
            partial_value.astype(jnp.bfloat16), "half", scatter_dimension=1, tiled=True
        )
        results = summed.reshape(experts, capacity, half_width)
        returned = lax.all_to_all(
            results, ("group", "member"), split_axis=0, concat_axis=0, tiled=True
        )
        select_table = (matches[:, :, :, None] & slot_table[:, None, :, :]).astype(jnp.bfloat16)
        select_table = select_table.reshape(block_rows, picks, experts * capacity)
        chosen_rows = jnp.einsum(
            "tks,sd->tkd",
            select_table,
            returned.reshape(experts * capacity, half_width),
            preferred_element_type=jnp.float32,
        )
        block_out = jnp.sum(weights[:, :, None] * chosen_rows, axis=1)
        return block_out.astype(jnp.bfloat16)

    outputs = lax.map(one_block, (token_blocks, id_blocks, gate_blocks))
    return outputs.reshape(tok_dev, half_width)


def solution(mesh):
    in_specs = (
        P(("parts", "group", "member"), "half"),
        P(),
        P(("group", "member"), None, "half"),
        P(("group", "member"), "half", None),
        P(("parts", "group", "member"), None),
        P(("parts", "group", "member"), None),
    )
    out_specs = P(("parts", "group", "member"), "half")
    return jax.shard_map(
        on_device, mesh=mesh, in_specs=in_specs, out_specs=out_specs, check_vma=False
    )
```

profile of v0, /device:TPU:0, one launch (start us, length us, event | category | flops | bytes accessed | tf_op | source)
XLA Modules:
  0.0 155.6 jit_solution(12856012240856181956)
XLA Ops:
  0.0 0.0 copy-start
  0.0 0.0 copy-start.1
  0.0 0.0 copy-start.2
  0.0 0.0 copy-start.3
  0.0 4.6 %copy.23 = bf16[1,1344,928]{2,1,0:T(8,128)(2,1)} copy(bf16[1,1344,928]{1,2,0:T(8,128)(2,1)} %param.10) | data formatting | bytes 4988928 | tf_op args[2]
  4.6 0.0 copy-done
  4.6 0.1 fusion.14
  4.8 0.0 copy-done.1
  4.8 0.1 fusion.16
  4.9 0.0 copy-done.2
  4.9 0.1 reshape.104
  5.0 0.0 copy-done.3
  5.0 0.1 reshape.105
  5.1 149.8 %while.10 = (s32[]{:T(128)}, bf16[2,32,1344]{2,1,0:T(8,128)(2,1)S(1)}, f32[2,32,6]{1,0,2:T(2,128)S(1)}, s32[2,32,6]{1,0,2:T(2,128)S(1)}, bf16[2,32,1344]{2,1,0:T...) while((s32[]{:T(128)}, ...), condition=%wide.region_5.6_spmd, body=%wide.region_1.5_spmd.sunk | while | flops 2149655552 | bytes 18970776 | solution.py:72
  5.1 0.1 copy.41
  5.2 0.1 reduce_window_sum.12
  5.3 0.1 copy.42
  5.4 0.1 copy.43
  5.5 0.5 convolution_convert_fusion.4
  6.0 1.2 copy.44
  7.2 35.2 %all_to_all.12 = bf16[16,24,1344]{2,1,0:T(8,128)(2,1)S(1)} all-to-all(bf16[16,24,1344]{2,1,0:T(8,128)(2,1)S(1)} %bitcast.65), channel_id=1, replica_groups=mesh['parts'=2,'group'=4,'member'=4,'half'=1] {'group','member'}, dimensions={0} | all-to-all | bytes 2064384 | tf_op jit(solution)/shard_map/while/body/eval_jaxpr/all_to_all | solution.py:44
  42.4 5.7 %convolution_convert_fusion.5 = bf16[384,1344]{0,1:T(8,128)(2,1)S(1)} fusion(bf16[928,1344]{1,0:T(8,128)(2,1)} %get-tuple-element.150, bf16[384,1344]{1,0:T(8,128)(2,1)S(1)} %bitcast.66, bf16[1344,928]{1,0:T(8,128)(2,1)} %get-tuple-element.149), kind=kOutput, calls=%fused_computation.1.clone.1 | convolution fusion | flops 1917333504 | bytes 7053312 | tf_op jit(solution)/shard_map/while/body/eval_jaxpr/dot_general | solution.py:50
  48.1 1.9 %copy.45 = bf16[384,1344]{1,0:T(8,128)(2,1)} copy(bf16[384,1344]{0,1:T(8,128)(2,1)S(1)} %convolution_convert_fusion.5) | data formatting | bytes 2064384 | tf_op jit(solution)/shard_map/while/body/eval_jaxpr/optimization_barrier | solution.py:53
  50.0 3.7 %all-to-all-start.1 = ((bf16[16,24,1344]{2,1,0:T(8,128)(2,1)}), bf16[16,24,1344]{2,1,0:T(8,128)(2,1)S(1)}, u32[]{:S(2)}, u32[]{:S(2)}) async-start(bf16[16,24,1344]{2,1,0:T(8,128)(2,1)} %bitcast.63), calls=%async_computation.1 | async-start | bytes 2162688 | tf_op jit(solution)/shard_map/while/body/eval_jaxpr/all_to_all | solution.py:58
  53.7 27.6 %all-to-all-done.1 = bf16[16,24,1344]{2,1,0:T(8,128)(2,1)S(1)} async-done(((bf16[16,24,1344]{2,1,0:T(8,128)(2,1)}), bf16[16,24,1344]{2,1,0:T(8,128)(2,1)S(1)}, u32[]{:S(2)}, u32[]{:S(2)}) %all-to-all-start.1) | async-done | bytes 1032224 | tf_op jit(solution)/shard_map/while/body/eval_jaxpr/all_to_all | solution.py:58
  81.3 0.7 fusion.38
  82.1 0.1 copy.41
  82.2 0.1 reduce_window_sum.12
  82.2 0.1 copy.42
  82.3 0.1 copy.43
  82.5 0.5 convolution_convert_fusion.4
  83.0 1.2 copy.44
  84.2 31.1 %all_to_all.12 = bf16[16,24,1344]{2,1,0:T(8,128)(2,1)S(1)} all-to-all(bf16[16,24,1344]{2,1,0:T(8,128)(2,1)S(1)} %bitcast.65), channel_id=1, replica_groups=mesh['parts'=2,'group'=4,'member'=4,'half'=1] {'group','member'}, dimensions={0} | all-to-all | bytes 2064384 | tf_op jit(solution)/shard_map/while/body/eval_jaxpr/all_to_all | solution.py:44
  115.3 5.7 %convolution_convert_fusion.5 = bf16[384,1344]{0,1:T(8,128)(2,1)S(1)} fusion(bf16[928,1344]{1,0:T(8,128)(2,1)} %get-tuple-element.150, bf16[384,1344]{1,0:T(8,128)(2,1)S(1)} %bitcast.66, bf16[1344,928]{1,0:T(8,128)(2,1)} %get-tuple-element.149), kind=kOutput, calls=%fused_computation.1.clone.1 | convolution fusion | flops 1917333504 | bytes 7053312 | tf_op jit(solution)/shard_map/while/body/eval_jaxpr/dot_general | solution.py:50
  121.0 1.9 %copy.45 = bf16[384,1344]{1,0:T(8,128)(2,1)} copy(bf16[384,1344]{0,1:T(8,128)(2,1)S(1)} %convolution_convert_fusion.5) | data formatting | bytes 2064384 | tf_op jit(solution)/shard_map/while/body/eval_jaxpr/optimization_barrier | solution.py:53
  122.9 3.7 %all-to-all-start.1 = ((bf16[16,24,1344]{2,1,0:T(8,128)(2,1)}), bf16[16,24,1344]{2,1,0:T(8,128)(2,1)S(1)}, u32[]{:S(2)}, u32[]{:S(2)}) async-start(bf16[16,24,1344]{2,1,0:T(8,128)(2,1)} %bitcast.63), calls=%async_computation.1 | async-start | bytes 2162688 | tf_op jit(solution)/shard_map/while/body/eval_jaxpr/all_to_all | solution.py:58
  126.6 27.6 %all-to-all-done.1 = bf16[16,24,1344]{2,1,0:T(8,128)(2,1)S(1)} async-done(((bf16[16,24,1344]{2,1,0:T(8,128)(2,1)}), bf16[16,24,1344]{2,1,0:T(8,128)(2,1)S(1)}, u32[]{:S(2)}, u32[]{:S(2)}) %all-to-all-start.1) | async-done | bytes 1032224 | tf_op jit(solution)/shard_map/while/body/eval_jaxpr/all_to_all | solution.py:58
  154.2 0.7 fusion.38
  154.9 0.0 copy-start.4
  154.9 0.7 copy-done.4
  (20 shorter events, 0.3 us)
Async XLA Ops:
  0.0 4.6 %copy-start = (bf16[64,1344]{1,0:T(8,128)(2,1)S(1)}, bf16[64,1344]{1,0:T(8,128)(2,1)}, u32[]{:S(2)}) copy-start(bf16[64,1344]{1,0:T(8,128)(2,1)} %param.8) | copy-start | bytes 516100
  0.0 4.8 %copy-start.1 = (f32[1344]{0:T(1024)S(1)}, f32[1344]{0:T(1024)}, u32[]{:S(2)}) copy-start(f32[1344]{0:T(1024)} %param.9) | copy-start | bytes 16132
  0.0 4.9 %copy-start.2 = (f32[64,6]{0,1:T(8,128)S(1)}, f32[64,6]{0,1:T(8,128)}, u32[]{:S(2)}) copy-start(f32[64,6]{0,1:T(8,128)} %param.13) | copy-start | bytes 4612
  0.0 5.0 %copy-start.3 = (s32[64,6]{0,1:T(8,128)S(1)}, s32[64,6]{0,1:T(8,128)}, u32[]{:S(2)}) copy-start(s32[64,6]{0,1:T(8,128)} %param.12) | copy-start | bytes 4612
  50.0 31.3 %all-to-all-start.1 = ((bf16[16,24,1344]{2,1,0:T(8,128)(2,1)}), bf16[16,24,1344]{2,1,0:T(8,128)(2,1)S(1)}, u32[]{:S(2)}, u32[]{:S(2)}) async-start(bf16[16,24,1344]{2,1,0:T(8,128)(2,1)} %bitcast.63), calls=%async_computation.1 | async-start | bytes 2162688 | tf_op jit(solution)/shard_map/while/body/eval_jaxpr/all_to_all | solution.py:58
  122.9 31.3 %all-to-all-start.1 = ((bf16[16,24,1344]{2,1,0:T(8,128)(2,1)}), bf16[16,24,1344]{2,1,0:T(8,128)(2,1)S(1)}, u32[]{:S(2)}, u32[]{:S(2)}) async-start(bf16[16,24,1344]{2,1,0:T(8,128)(2,1)} %bitcast.63), calls=%async_computation.1 | async-start | bytes 2162688 | tf_op jit(solution)/shard_map/while/body/eval_jaxpr/all_to_all | solution.py:58
  154.9 0.7 copy-start.4
where the time goes:
time: 156 us
  blocking collectives  66.3 us (42%)
  waiting for transfers between devices  55.2 us (35%)
  matrix products  13.7 us (9%)
  local copies, waits for them, and re-layouts  12.2 us (8%)
  starting transfers between devices  7.39 us (5%)
    all_to_all x2, blocking collectives, one_block(): lax.all_to_all(outgoing, ('group', 'member'), split_axis=0, concat_axis=0...  66.3 us
    all_to_all x2, waiting for transfers between devices, one_block(): lax.all_to_all(results, ('group', 'member'), split_axis=0, concat_axis=0,...  55.2 us
    dot_general x2, matrix products, one_block(): jnp.dot(hidden, down_local, preferred_element_type=jnp.float32)  11.4 us
    all_to_all x2, starting transfers between devices, one_block(): lax.all_to_all(results, ('group', 'member'), split_axis=0, concat_axis=0,...  7.39 us
    unnamed x11, local copies, waits for them, and re-layouts  5.29 us
    optimization_barrier x2, local copies, waits for them, and re-layouts, one_block(): partial_value = lax.optimization_barrier(partial_value).astype(jnp.float32)  3.82 us
  transfers between devices with their start and end apart: 2, of which 2 were waited for; matrix products, arithmetic and copies ran while one was open for 0% of the time, Pallas kernels for 0%

commit v1 on v0

--- a/solution.py
+++ b/solution.py
@@ -1,15 +1,393 @@
+import functools
+
 import jax
 import jax.numpy as jnp
 from jax import lax
+from jax.experimental import pallas as pl
+from jax.experimental.pallas import tpu as pltpu
 from jax.sharding import PartitionSpec as P
 
 MB_TOK = 32
-
+LANES = 128
 
 epsilon = 1e-05
 
 
-def on_device(tokens, norm_gain, w_up, w_down, expert_ids, gates):
+def visiting_orders(members):
+    middle = (members - 1) / 2
+    return [
+        sorted(range(members), key=lambda s: (abs(s - m), abs(s - middle)))
+        for m in range(members)
+    ]
+
+
+def fused_kernel(
+    members,
+    tok_ref,
+    gain_ref,
+    ids_ref,
+    gates_ref,
+    up_hbm,
+    down_hbm,
+    out_ref,
+    gathered,
+    up_ref,
+    down_ref,
+    partials,
+    core_in,
+    core_sum,
+    x_in,
+    chain_out,
+    chain_in,
+    w_sem,
+    ag_send,
+    ag_recv,
+    own_send,
+    core_send,
+    core_recv,
+    x_send,
+    x_recv,
+    chain_send,
+    chain_recv,
+):
+    rows, width = tok_ref.shape
+    picks = ids_ref.shape[1]
+    padded = gathered.shape[2]
+    base = width // LANES * LANES
+    off = width - base
+    part = lax.axis_index("parts")
+    g = lax.axis_index("group")
+    m = lax.axis_index("member")
+    half = lax.axis_index("half")
+    experts = lax.axis_size("group") * members
+    me = g * members + m
+    core_peer = (part, g + 1 - 2 * lax.rem(g, 2), m, half)
+    x_peer = (part, lax.rem(g + 2, 4), m, half)
+    has_left = m > 0
+    has_right = m < members - 1
+
+    def chain_peer(place):
+        return (part, g, place, half)
+
+    up_copy = pltpu.make_async_copy(up_hbm.at[0], up_ref.at[pl.ds(0, width), :], w_sem.at[0])
+    down_copy = pltpu.make_async_copy(down_hbm.at[0], down_ref, w_sem.at[1])
+    up_copy.start()
+    down_copy.start()
+
+    barrier = pltpu.get_barrier_semaphore()
+
+    def greet(peer):
+        pl.semaphore_signal(barrier, inc=1, device_id=peer, device_id_type=pl.DeviceIdType.MESH)
+
+    greet(core_peer)
+    greet(x_peer)
+
+    @pl.when(has_left)
+    def _():
+        greet(chain_peer(m - 1))
+
+    @pl.when(has_right)
+    def _():
+        greet(chain_peer(m + 1))
+
+    block = padded - base
+    lane = lax.broadcasted_iota(jnp.int32, (rows, block), 1) - off
+    piece = (lane >= experts).astype(jnp.int32) + (lane >= 2 * experts).astype(jnp.int32)
+    lane_expert = lane - piece * experts
+    weight = jnp.zeros((rows, block), jnp.float32)
+    for k in range(picks):
+        weight += jnp.where(lane_expert == ids_ref[:, k : k + 1], gates_ref[:, k : k + 1], 0.0)
+    high = weight.astype(jnp.bfloat16).astype(jnp.float32)
+    rest = weight - high
+    middle = rest.astype(jnp.bfloat16).astype(jnp.float32)
+    low = rest - middle
+    pieces = jnp.where(piece == 0, high, jnp.where(piece == 1, middle, low))
+    values = tok_ref[...].astype(jnp.float32)
+    inverse_rms = lax.rsqrt(jnp.mean(values * values, axis=-1, keepdims=True) + epsilon)
+    normed = (values * inverse_rms * gain_ref[...]).astype(jnp.bfloat16)
+    own_rows = pl.ds(0, rows)
+    gathered[m, own_rows, base:padded] = jnp.zeros((rows, block), jnp.bfloat16)
+    gathered[m, own_rows, 0:width] = normed
+    tail = gathered[m, own_rows, base:padded].astype(jnp.float32)
+    gathered[m, own_rows, base:padded] = jnp.where(lane < 0, tail, pieces).astype(jnp.bfloat16)
+    up_ref[pl.ds(width, padded - width), :] = jnp.zeros((padded - width, up_ref.shape[1]), jnp.bfloat16)
+
+    pl.semaphore_wait(barrier, 2 + has_left.astype(jnp.int32) + has_right.astype(jnp.int32))
+
+    def gather_copy(s, source, target, peer, send):
+        return pltpu.make_async_remote_copy(
+            src_ref=gathered.at[s, pl.ds(source * rows, rows), :],
+            dst_ref=gathered.at[s, pl.ds(target * rows, rows), :],
+            send_sem=send,
+            recv_sem=ag_recv.at[target, s],
+            device_id=peer,
+            device_id_type=pl.DeviceIdType.MESH,
+        )
+
+    def to_chain(s, place):
+        return gather_copy(s, 0, 0, chain_peer(place), ag_send.at[0, s])
+
+    def to_left_first():
+        return gather_copy(m, 0, 0, chain_peer(m - 1), own_send.at[0])
+
+    def to_right_first():
+        return gather_copy(m, 0, 0, chain_peer(m + 1), own_send.at[1])
+
+    def to_x(s):
+        return gather_copy(s, 0, 1, x_peer, ag_send.at[1, s])
+
+    def to_core(s):
+        return gather_copy(s, 0, 2, core_peer, ag_send.at[2, s])
+
+    def to_core_far(s):
+        return gather_copy(s, 1, 3, core_peer, ag_send.at[3, s])
+
+    @pl.when(has_left)
+    def _():
+        to_left_first().start()
+
+    @pl.when(has_right)
+    def _():
+        to_right_first().start()
+
+    to_x(m).start()
+    to_core(m).start()
+
+    orders = visiting_orders(members)
+
+    def place_at(i):
+        code = m * members + i
+        found = jnp.int32(0)
+        for a in range(members):
+            for b in range(members):
+                found = found + jnp.where(code == a * members + b, orders[a][b], 0)
+        return found
+
+    def pass_on(s, next_place, goes_on):
+        to_chain(s, next_place).wait_recv()
+
+        @pl.when(goes_on)
+        def _():
+            to_chain(s, next_place).start()
+
+        to_x(s).start()
+        to_core(s).start()
+
+    def core_copy(s):
+        return pltpu.make_async_remote_copy(
+            src_ref=partials.at[s, pl.ds(2 * rows, 2 * rows), :],
+            dst_ref=core_in.at[s],
+            send_sem=core_send.at[s],
+            recv_sem=core_recv.at[s],
+            device_id=core_peer,
+            device_id_type=pl.DeviceIdType.MESH,
+        )
+
+    def x_copy(s):
+        return pltpu.make_async_remote_copy(
+            src_ref=core_sum.at[s, pl.ds(rows, rows), :],
+            dst_ref=x_in.at[s],
+            send_sem=x_send.at[s],
+            recv_sem=x_recv.at[s],
+            device_id=x_peer,
+            device_id_type=pl.DeviceIdType.MESH,
+        )
+
+    def chain_copy(s, side, place):
+        return pltpu.make_async_remote_copy(
+            src_ref=chain_out.at[s],
+            dst_ref=chain_in.at[side, s],
+            send_sem=chain_send.at[s],
+            recv_sem=chain_recv.at[side, s],
+            device_id=chain_peer(place),
+            device_id_type=pl.DeviceIdType.MESH,
+        )
+
+    all_lane = lax.broadcasted_iota(jnp.int32, (4 * rows, block), 1) - off
+    mine = (all_lane == me) | (all_lane == me + experts) | (all_lane == me + 2 * experts)
+
+    def gather_step(i, carry):
+        left = m - i - 1
+        right = m + i + 1
+
+        @pl.when(left >= 0)
+        def _():
+            pass_on(left, m + 1, has_right)
+
+        @pl.when(right < members)
+        def _():
+            pass_on(right, m - 1, has_left)
+
+        s = place_at(i)
+        to_x(s).wait_recv()
+        to_core_far(s).start()
+        to_core(s).wait_recv()
+        to_core_far(s).wait_recv()
+
+        @pl.when(i == 0)
+        def _():
+            up_copy.wait()
+            down_copy.wait()
+
+        tail_block = gathered[s, :, base:padded].astype(jnp.float32)
+        row_weight = jnp.sum(jnp.where(mine, tail_block, 0.0), axis=1, keepdims=True)
+        up_values = jnp.dot(gathered[s], up_ref[...], preferred_element_type=jnp.float32)
+        hidden = jnp.square(jnp.maximum(up_values, 0.0)).astype(jnp.bfloat16)
+        down_values = jnp.dot(hidden, down_ref[...], preferred_element_type=jnp.float32)
+        partials[s] = (down_values * row_weight).astype(jnp.bfloat16)
+        core_copy(s).start()
+        return carry
+
+    lax.fori_loop(0, members, gather_step, 0)
+
+    def add(a, b):
+        return a.astype(jnp.float32) + b.astype(jnp.float32)
+
+    def core_step(i, carry):
+        s = place_at(members - 1 - i)
+        core_copy(s).wait_recv()
+        far = pl.ds(rows, rows)
+        core_sum[s, far, :] = add(partials[s, far, :], core_in[s, far, :]).astype(jnp.bfloat16)
+        x_copy(s).start()
+        return carry
+
+    lax.fori_loop(0, members, core_step, 0)
+
+    def own_sum(s):
+        x_copy(s).wait_recv()
+        return add(partials[s, own_rows, :], core_in[s, own_rows, :]) + x_in[s].astype(jnp.float32)
+
+    def chain_step(i, carry):
+        s = place_at(members - 1 - i)
+        total = own_sum(s)
+
+        def onward(side, upstream, next_place):
+            @pl.when(upstream)
+            def _():
+                chain_copy(s, side, next_place).wait_recv()
+                chain_out[s] = (total + chain_in[side, s].astype(jnp.float32)).astype(jnp.bfloat16)
+
+            @pl.when(jnp.logical_not(upstream))
+            def _():
+                chain_out[s] = total.astype(jnp.bfloat16)
+
+            chain_copy(s, side, next_place).start()
+
+        @pl.when(s > m)
+        def _():
+            onward(0, has_left, m + 1)
+
+        @pl.when(s < m)
+        def _():
+            onward(1, has_right, m - 1)
+
+        return carry
+
+    lax.fori_loop(0, members - 1, chain_step, 0)
+
+    total = own_sum(m)
+
+    @pl.when(has_left & has_right)
+    def _():
+        chain_copy(m, 0, m + 1).wait_recv()
+        chain_copy(m, 1, m - 1).wait_recv()
+        both = add(chain_in[0, m], chain_in[1, m])
+        out_ref[...] = (total + both).astype(out_ref.dtype)
+
+    @pl.when(has_left & jnp.logical_not(has_right))
+    def _():
+        chain_copy(m, 0, m - 1).wait_recv()
+        out_ref[...] = (total + chain_in[0, m].astype(jnp.float32)).astype(out_ref.dtype)
+
+    @pl.when(has_right & jnp.logical_not(has_left))
+    def _():
+        chain_copy(m, 1, m + 1).wait_recv()
+        out_ref[...] = (total + chain_in[1, m].astype(jnp.float32)).astype(out_ref.dtype)
+
+    @pl.when(has_left)
+    def _():
+        to_left_first().wait_send()
+
+    @pl.when(has_right)
+    def _():
+        to_right_first().wait_send()
+
+    def finish(s, carry):
+        to_x(s).wait_send()
+        to_core(s).wait_send()
+        to_core_far(s).wait_send()
+        core_copy(s).wait_send()
+        x_copy(s).wait_send()
+
+        @pl.when((s < m) & has_right)
+        def _():
+            to_chain(s, m + 1).wait_send()
+
+        @pl.when((s > m) & has_left)
+        def _():
+            to_chain(s, m - 1).wait_send()
+
+        @pl.when(s > m)
+        def _():
+            chain_copy(s, 0, m + 1).wait_send()
+
+        @pl.when(s < m)
+        def _():
+            chain_copy(s, 1, m - 1).wait_send()
+
+        return carry
+
+    lax.fori_loop(0, members, finish, 0)
+
+
+def fused_on_device(tokens, norm_gain, w_up, w_down, expert_ids, gates):
+    members = lax.axis_size("member")
+    experts = lax.axis_size("group") * members
+    rows, width = tokens.shape
+    hidden_width = w_up.shape[2]
+    padded = -(-(width + 3 * experts) // LANES) * LANES
+    vmem = pl.BlockSpec(memory_space=pltpu.VMEM)
+    hbm = pl.BlockSpec(memory_space=pl.ANY)
+    dma = pltpu.SemaphoreType.DMA
+    total_rows = 4 * members * rows
+    return pl.pallas_call(
+        functools.partial(fused_kernel, members),
+        out_shape=jax.ShapeDtypeStruct((rows, width), jnp.bfloat16),
+        in_specs=[vmem, vmem, vmem, vmem, hbm, hbm],
+        out_specs=vmem,
+        scratch_shapes=[
+            pltpu.VMEM((members, 4 * rows, padded), jnp.bfloat16),
+            pltpu.VMEM((padded, hidden_width), jnp.bfloat16),
+            pltpu.VMEM((hidden_width, width), jnp.bfloat16),
+            pltpu.VMEM((members, 4 * rows, width), jnp.bfloat16),
+            pltpu.VMEM((members, 2 * rows, width), jnp.bfloat16),
+            pltpu.VMEM((members, 2 * rows, width), jnp.bfloat16),
+            pltpu.VMEM((members, rows, width), jnp.bfloat16),
+            pltpu.VMEM((members, rows, width), jnp.bfloat16),
+            pltpu.VMEM((2, members, rows, width), jnp.bfloat16),
+            dma((2,)),
+            dma((4, members)),
+            dma((4, members)),
+            dma((2,)),
+            dma((members,)),
+            dma((members,)),
+            dma((members,)),
+            dma((members,)),
+            dma((members,)),
+            dma((2, members)),
+        ],
+        compiler_params=pltpu.CompilerParams(
+            collective_id=0, has_side_effects=True, vmem_limit_bytes=48 * 2**20
+        ),
+        cost_estimate=pl.CostEstimate(
+            flops=4 * total_rows * width * hidden_width,
+            bytes_accessed=4 * width * hidden_width,
+            transcendentals=0,
+        ),
+    )(tokens, norm_gain.reshape(1, width), expert_ids, gates, w_up, w_down)
+
+
+def routed_on_device(tokens, norm_gain, w_up, w_down, expert_ids, gates):
     groups = lax.axis_size("group")
     members = lax.axis_size("member")
     experts = groups * members
@@ -27,15 +405,19 @@
     token_blocks = normed.reshape(micro_count, block_rows, normed.shape[1])
     id_blocks = expert_ids.reshape(micro_count, block_rows, picks)
     gate_blocks = gates.reshape(micro_count, block_rows, picks)
+    row_iota = jnp.arange(block_rows, dtype=jnp.int32)
+    earlier = (row_iota[:, None] > row_iota[None, :]).astype(jnp.bfloat16)
 
     def one_block(pieces):
         block_tokens, block_ids, weights = pieces
         expert_iota = jnp.arange(experts, dtype=jnp.int32)
         matches = block_ids[:, :, None] == expert_iota[None, None, :]
-        picked = jnp.any(matches, axis=1).astype(jnp.int32)
-        before = jnp.cumsum(picked, axis=0) - picked
+        picked = jnp.any(matches, axis=1)
+        before = jnp.dot(
+            earlier, picked.astype(jnp.bfloat16), preferred_element_type=jnp.float32
+        ).astype(jnp.int32)
         slot_iota = jnp.arange(capacity, dtype=jnp.int32)
-        slot_table = (picked[:, :, None] == 1) & (before[:, :, None] == slot_iota[None, None, :])
+        slot_table = picked[:, :, None] & (before[:, :, None] == slot_iota[None, None, :])
         slot_bf = slot_table.astype(jnp.bfloat16).reshape(block_rows, experts * capacity)
         outgoing = lax.dot_general(
             slot_bf, block_tokens, (((0,), (0,)), ((), ())), preferred_element_type=jnp.float32
@@ -83,6 +465,8 @@
         P(("parts", "group", "member"), None),
     )
     out_specs = P(("parts", "group", "member"), "half")
+    fused = mesh.shape["half"] == 1 and mesh.shape["group"] == 4 and 1 < mesh.shape["member"] <= 4
+    on_device = fused_on_device if fused else routed_on_device
     return jax.shard_map(
         on_device, mesh=mesh, in_specs=in_specs, out_specs=out_specs, check_vma=False
     )

time: 156 us -> 62.3 us (0.40)
  blocking collectives: 66.3 us -> 0 us
  waiting for transfers between devices: 55.2 us -> 0 us
  Pallas kernels: 0 us -> 54 us
  matrix products: 13.7 us -> 0 us
  starting transfers between devices: 7.39 us -> 0 us
  local copies, waits for them, and re-layouts: 12.2 us -> 7.97 us
    all_to_all x2 -> x0, blocking collectives: 66.3 us -> none  [one_block(): lax.all_to_all(outgoing, ('group', 'member'), split_axis=0, concat_axis=0...]
    all_to_all x2 -> x0, waiting for transfers between devices: 55.2 us -> none  [one_block(): lax.all_to_all(results, ('group', 'member'), split_axis=0, concat_axis=0,...]
    pallas_call x0 -> x1, Pallas kernels: none -> 54 us  [fused_on_device(): pl.pallas_call(functools.partial(fused_kernel, members), out_shape=jax.Sh...]
    dot_general x6 -> x0, matrix products: 13.7 us -> none  [the longest x2 11.4 us: one_block(): jnp.dot(hidden, down_local, preferred_element_type=jnp.float32)]
    all_to_all x2 -> x0, starting transfers between devices: 7.39 us -> none  [one_block(): lax.all_to_all(results, ('group', 'member'), split_axis=0, concat_axis=0,...]
    optimization_barrier x2 -> x0, local copies, waits for them, and re-layouts: 3.82 us -> none  [one_block(): partial_value = lax.optimization_barrier(partial_value).astype(jnp.float32)]
    convert_element_type x2 -> x0, local copies, waits for them, and re-layouts: 2.4 us -> none  [one_block(): outgoing.astype(jnp.bfloat16)]
    unnamed x11 -> x8, local copies, waits for them, and re-layouts: 5.29 us -> 7.27 us
  transfers between devices with their start and end apart: 2 -> 0, of which waited for: 2 -> 0; matrix products, arithmetic and copies ran while one was open for 0% -> 0% of each run, Pallas kernels for 0% -> 0%
where the time goes in v1:
time: 62.3 us; the launch traced here: 62 us
  Pallas kernels  54 us (87%)
  local copies, waits for them, and re-layouts  7.97 us (13%)
    pallas_call x1, Pallas kernels, fused_on_device(): pl.pallas_call(functools.partial(fused_kernel, members), out_shape=jax.Sh...  54 us
    unnamed x8, local copies, waits for them, and re-layouts  7.27 us

profile of v1, /device:TPU:0, one launch (start us, length us, event | category | flops | bytes accessed | tf_op | source)
XLA Modules:
  0.0 62.0 jit_solution(17821532124109241476)
XLA Ops:
  0.0 0.7 %reshape.3.gain_ref = f32[1,1344]{1,0:T(1,128)S(1)} reshape(f32[1344]{0:T(1024)} %param.7) | data formatting | bytes 10752 | tf_op jit(solution)/shard_map/reshape | solution.py:387
  0.7 0.8 %copy.7.ids_ref = s32[64,6]{1,0:T(8,128)S(1)} copy(s32[64,6]{0,1:T(8,128)} %param.10) | data formatting | bytes 3072 | tf_op args[4]
  1.5 0.8 %copy.8.gates_ref = f32[64,6]{1,0:T(8,128)S(1)} copy(f32[64,6]{0,1:T(8,128)} %param.11) | data formatting | bytes 3072 | tf_op args[5]
  2.3 0.0 copy-start.1
  2.3 3.3 %copy.9.up_hbm = bf16[1,1344,928]{2,1,0:T(8,128)(2,1)S(1)} copy(bf16[1,1344,928]{1,2,0:T(8,128)(2,1)} %param.8) | data formatting | bytes 4988928 | tf_op args[2]
  5.6 0.0 copy-done.1
  5.6 0.0 copy-start
  5.6 1.7 %copy-done = bf16[1,928,1344]{2,1,0:T(8,128)(2,1)S(1)} copy-done((bf16[1,928,1344]{2,1,0:T(8,128)(2,1)S(1)}, bf16[1,928,1344]{2,1,0:T(8,128)(2,1)}, u32[]{:S(2)}) %copy-start) | copy-done | bytes 2494488
  7.3 54.0 %shard_map.64 = bf16[64,1344]{1,0:T(8,128)(2,1)S(1)} custom-call(bf16[64,1344]{1,0:T(8,128)(2,1)S(1)} %copy-done.1, f32[1,1344]{1,0:T(1,128)S(1)} %reshape.3.gain_ref, s32[64,6]{1,0:T(8,128)S(1)} %copy.7.ids_ref, f32[64,6]{1,0:T(8,128)S(1)} %copy.8.gates_ref, bf16[1,1344,928]{2,1,0:T(8,128)(2,1)S(1)} %copy.9.up_hbm, bf16[1,928,1344]{2,1,0:T(8,128)(2,1)S(1)} %copy-done), custom_call_target="tpu_custom_call" | custom-call | flops 5108662272 | bytes 4988928 | tf_op jit(solution)/shard_map/pallas_call | solution.py:353
  61.3 0.7 %copy.11 = bf16[64,1344]{1,0:T(8,128)(2,1)} copy(bf16[64,1344]{1,0:T(8,128)(2,1)S(1)} %shard_map.64) | data formatting | bytes 344064
Async XLA Ops:
  2.3 3.3 %copy-start.1 = (bf16[64,1344]{1,0:T(8,128)(2,1)S(1)}, bf16[64,1344]{1,0:T(8,128)(2,1)}, u32[]{:S(2)}) copy-start(bf16[64,1344]{1,0:T(8,128)(2,1)} %tok_ref.1) | copy-start | bytes 516100
  5.6 1.7 %copy-start = (bf16[1,928,1344]{2,1,0:T(8,128)(2,1)S(1)}, bf16[1,928,1344]{2,1,0:T(8,128)(2,1)}, u32[]{:S(2)}) copy-start(bf16[1,928,1344]{2,1,0:T(8,128)(2,1)} %down_hbm.1) | copy-start | bytes 7483396

commit v2 on v1

--- a/solution.py
+++ b/solution.py
@@ -51,7 +51,7 @@
     chain_recv,
 ):
     rows, width = tok_ref.shape
-    picks = ids_ref.shape[1]
+    picks = ids_ref.shape[0]
     padded = gathered.shape[2]
     base = width // LANES * LANES
     off = width - base
@@ -69,7 +69,7 @@
     def chain_peer(place):
         return (part, g, place, half)
 
-    up_copy = pltpu.make_async_copy(up_hbm.at[0], up_ref.at[pl.ds(0, width), :], w_sem.at[0])
+    up_copy = pltpu.make_async_copy(up_hbm.at[0], up_ref, w_sem.at[0])
     down_copy = pltpu.make_async_copy(down_hbm.at[0], down_ref, w_sem.at[1])
     up_copy.start()
     down_copy.start()
@@ -91,26 +91,26 @@
         greet(chain_peer(m + 1))
 
     block = padded - base
-    lane = lax.broadcasted_iota(jnp.int32, (rows, block), 1) - off
-    piece = (lane >= experts).astype(jnp.int32) + (lane >= 2 * experts).astype(jnp.int32)
-    lane_expert = lane - piece * experts
-    weight = jnp.zeros((rows, block), jnp.float32)
+    spot = lax.broadcasted_iota(jnp.int32, (block, rows), 0) - off
+    piece = (spot >= experts).astype(jnp.int32) + (spot >= 2 * experts).astype(jnp.int32)
+    spot_expert = spot - piece * experts
+    weight = jnp.zeros((block, rows), jnp.float32)
     for k in range(picks):
-        weight += jnp.where(lane_expert == ids_ref[:, k : k + 1], gates_ref[:, k : k + 1], 0.0)
+        weight += jnp.where(spot_expert == ids_ref[k : k + 1, :], gates_ref[k : k + 1, :], 0.0)
     high = weight.astype(jnp.bfloat16).astype(jnp.float32)
     rest = weight - high
     middle = rest.astype(jnp.bfloat16).astype(jnp.float32)
     low = rest - middle
-    pieces = jnp.where(piece == 0, high, jnp.where(piece == 1, middle, low))
+    pieces = jnp.where(piece == 0, high, jnp.where(piece == 1, middle, low)).T
+    lane = lax.broadcasted_iota(jnp.int32, (rows, block), 1) - off
     values = tok_ref[...].astype(jnp.float32)
     inverse_rms = lax.rsqrt(jnp.mean(values * values, axis=-1, keepdims=True) + epsilon)
-    normed = (values * inverse_rms * gain_ref[...]).astype(jnp.bfloat16)
+    normed = (values * inverse_rms * gain_ref[...].reshape(1, width)).astype(jnp.bfloat16)
     own_rows = pl.ds(0, rows)
     gathered[m, own_rows, base:padded] = jnp.zeros((rows, block), jnp.bfloat16)
     gathered[m, own_rows, 0:width] = normed
     tail = gathered[m, own_rows, base:padded].astype(jnp.float32)
     gathered[m, own_rows, base:padded] = jnp.where(lane < 0, tail, pieces).astype(jnp.bfloat16)
-    up_ref[pl.ds(width, padded - width), :] = jnp.zeros((padded - width, up_ref.shape[1]), jnp.bfloat16)
 
     pl.semaphore_wait(barrier, 2 + has_left.astype(jnp.int32) + has_right.astype(jnp.int32))
 
@@ -231,7 +231,12 @@
 
         tail_block = gathered[s, :, base:padded].astype(jnp.float32)
         row_weight = jnp.sum(jnp.where(mine, tail_block, 0.0), axis=1, keepdims=True)
-        up_values = jnp.dot(gathered[s], up_ref[...], preferred_element_type=jnp.float32)
+        up_values = lax.dot_general(
+            gathered[s, :, 0:width],
+            up_ref[...],
+            (((1,), (1,)), ((), ())),
+            preferred_element_type=jnp.float32,
+        )
         hidden = jnp.square(jnp.maximum(up_values, 0.0)).astype(jnp.bfloat16)
         down_values = jnp.dot(hidden, down_ref[...], preferred_element_type=jnp.float32)
         partials[s] = (down_values * row_weight).astype(jnp.bfloat16)
@@ -357,7 +362,7 @@
         out_specs=vmem,
         scratch_shapes=[
             pltpu.VMEM((members, 4 * rows, padded), jnp.bfloat16),
-            pltpu.VMEM((padded, hidden_width), jnp.bfloat16),
+            pltpu.VMEM((hidden_width, width), jnp.bfloat16),
             pltpu.VMEM((hidden_width, width), jnp.bfloat16),
             pltpu.VMEM((members, 4 * rows, width), jnp.bfloat16),
             pltpu.VMEM((members, 2 * rows, width), jnp.bfloat16),
@@ -377,14 +382,14 @@
             dma((2, members)),
         ],
         compiler_params=pltpu.CompilerParams(
-            collective_id=0, has_side_effects=True, vmem_limit_bytes=48 * 2**20
+            collective_id=0, has_side_effects=True, vmem_limit_bytes=60 * 2**20
         ),
         cost_estimate=pl.CostEstimate(
             flops=4 * total_rows * width * hidden_width,
             bytes_accessed=4 * width * hidden_width,
             transcendentals=0,
         ),
-    )(tokens, norm_gain.reshape(1, width), expert_ids, gates, w_up, w_down)
+    )(tokens, norm_gain, expert_ids.T, gates.T, jnp.swapaxes(w_up, 1, 2), w_down)
 
 
 def routed_on_device(tokens, norm_gain, w_up, w_down, expert_ids, gates):

time: 62.3 us -> 56.6 us (0.909)
  local copies, waits for them, and re-layouts: 7.97 us -> 1.61 us
  Pallas kernels: 54 us -> 54.8 us
    unnamed x8 -> x1, local copies, waits for them, and re-layouts: 7.27 us -> 1.61 us
    pallas_call x1, Pallas kernels: 54 us -> 54.8 us  [fused_on_device(): pl.pallas_call(functools.partial(fused_kernel, members), out_shape=jax.Sh...]
    reshape x1 -> x0, local copies, waits for them, and re-layouts: 0.7 us -> none  [fused_on_device(): norm_gain.reshape(1, width)]
where the time goes in v2:
time: 56.6 us; the launch traced here: 56.5 us
  Pallas kernels  54.8 us (97%)
  local copies, waits for them, and re-layouts  1.61 us (3%)
    pallas_call x1, Pallas kernels, fused_on_device(): pl.pallas_call(functools.partial(fused_kernel, members), out_shape=jax.Sh...  54.8 us
    unnamed x1, local copies, waits for them, and re-layouts  1.61 us

profile of v2, /device:TPU:0, one launch (start us, length us, event | category | flops | bytes accessed | tf_op | source)
XLA Modules:
  0.0 56.5 jit_solution(15071436457373680504)
XLA Ops:
  0.0 54.8 %shard_map.64 = bf16[64,1344]{1,0:T(8,128)(2,1)} custom-call(bf16[64,1344]{1,0:T(8,128)(2,1)} %tok_ref.1, f32[1344]{0:T(1024)} %gain_ref.1, s32[6,64]{1,0:T(8,128)} %bitcast.4, f32[6,64]{1,0:T(8,128)} %bitcast.5, bf16[1,928,1344]{2,1,0:T(8,128)(2,1)} %bitcast.3, bf16[1,928,1344]{2,1,0:T(8,128)(2,1)} %down_hbm.1), custom_call_target="tpu_custom_call" | custom-call | flops 5108662272 | bytes 4988928 | tf_op jit(solution)/shard_map/pallas_call | solution.py:358
  54.9 1.6 %copy.8 = bf16[64,1344]{1,0:T(8,128)(2,1)} copy(bf16[64,1344]{1,0:T(8,128)(2,1)} %shard_map.64) | data formatting | bytes 344064

commit v3 on v2

--- a/solution.py
+++ b/solution.py
@@ -9,6 +9,7 @@
 
 MB_TOK = 32
 LANES = 128
+PIECES = 4
 
 epsilon = 1e-05
 
@@ -19,6 +20,14 @@
         sorted(range(members), key=lambda s: (abs(s - m), abs(s - middle)))
         for m in range(members)
     ]
+
+
+def return_orders(members):
+    crossing, onward = [], []
+    for m, order in enumerate(visiting_orders(members)):
+        crossing.append([order[1]] + [s for s in order[::-1] if s != order[1]])
+        onward.append(crossing[-1] if m in (0, members - 1) else order[::-1])
+    return crossing, onward
 
 
 def fused_kernel(
@@ -53,6 +62,7 @@
     rows, width = tok_ref.shape
     picks = ids_ref.shape[0]
     padded = gathered.shape[2]
+    piece_rows = rows // PIECES
     base = width // LANES * LANES
     off = width - base
     part = lax.axis_index("parts")
@@ -92,8 +102,8 @@
 
     block = padded - base
     spot = lax.broadcasted_iota(jnp.int32, (block, rows), 0) - off
-    piece = (spot >= experts).astype(jnp.int32) + (spot >= 2 * experts).astype(jnp.int32)
-    spot_expert = spot - piece * experts
+    kind = (spot >= experts).astype(jnp.int32) + (spot >= 2 * experts).astype(jnp.int32)
+    spot_expert = spot - kind * experts
     weight = jnp.zeros((block, rows), jnp.float32)
     for k in range(picks):
         weight += jnp.where(spot_expert == ids_ref[k : k + 1, :], gates_ref[k : k + 1, :], 0.0)
@@ -101,7 +111,7 @@
     rest = weight - high
     middle = rest.astype(jnp.bfloat16).astype(jnp.float32)
     low = rest - middle
-    pieces = jnp.where(piece == 0, high, jnp.where(piece == 1, middle, low)).T
+    pieces = jnp.where(kind == 0, high, jnp.where(kind == 1, middle, low)).T
     lane = lax.broadcasted_iota(jnp.int32, (rows, block), 1) - off
     values = tok_ref[...].astype(jnp.float32)
     inverse_rms = lax.rsqrt(jnp.mean(values * values, axis=-1, keepdims=True) + epsilon)
@@ -114,48 +124,48 @@
 
     pl.semaphore_wait(barrier, 2 + has_left.astype(jnp.int32) + has_right.astype(jnp.int32))
 
-    def gather_copy(s, source, target, peer, send):
+    def gather_copy(s, h, source, target, peer, send):
         return pltpu.make_async_remote_copy(
-            src_ref=gathered.at[s, pl.ds(source * rows, rows), :],
-            dst_ref=gathered.at[s, pl.ds(target * rows, rows), :],
+            src_ref=gathered.at[s, pl.ds(source * rows + h * piece_rows, piece_rows), :],
+            dst_ref=gathered.at[s, pl.ds(target * rows + h * piece_rows, piece_rows), :],
             send_sem=send,
-            recv_sem=ag_recv.at[target, s],
+            recv_sem=ag_recv.at[target, s, h],
             device_id=peer,
             device_id_type=pl.DeviceIdType.MESH,
         )
 
-    def to_chain(s, place):
-        return gather_copy(s, 0, 0, chain_peer(place), ag_send.at[0, s])
-
-    def to_left_first():
-        return gather_copy(m, 0, 0, chain_peer(m - 1), own_send.at[0])
-
-    def to_right_first():
-        return gather_copy(m, 0, 0, chain_peer(m + 1), own_send.at[1])
-
-    def to_x(s):
-        return gather_copy(s, 0, 1, x_peer, ag_send.at[1, s])
-
-    def to_core(s):
-        return gather_copy(s, 0, 2, core_peer, ag_send.at[2, s])
-
-    def to_core_far(s):
-        return gather_copy(s, 1, 3, core_peer, ag_send.at[3, s])
-
-    @pl.when(has_left)
-    def _():
-        to_left_first().start()
-
-    @pl.when(has_right)
-    def _():
-        to_right_first().start()
-
-    to_x(m).start()
-    to_core(m).start()
-
-    orders = visiting_orders(members)
-
-    def place_at(i):
+    def to_chain(s, h, place):
+        return gather_copy(s, h, 0, 0, chain_peer(place), ag_send.at[0, s, h])
+
+    def to_left_first(h):
+        return gather_copy(m, h, 0, 0, chain_peer(m - 1), own_send.at[0, h])
+
+    def to_right_first(h):
+        return gather_copy(m, h, 0, 0, chain_peer(m + 1), own_send.at[1, h])
+
+    def to_x(s, h):
+        return gather_copy(s, h, 0, 1, x_peer, ag_send.at[1, s, h])
+
+    def to_core(s, h):
+        return gather_copy(s, h, 0, 2, core_peer, ag_send.at[2, s, h])
+
+    def to_core_far(s, h):
+        return gather_copy(s, h, 1, 3, core_peer, ag_send.at[3, s, h])
+
+    for h in range(PIECES):
+
+        @pl.when(has_left)
+        def _():
+            to_left_first(h).start()
+
+        @pl.when(has_right)
+        def _():
+            to_right_first(h).start()
+
+        to_x(m, h).start()
+        to_core(m, h).start()
+
+    def looked_up(orders, i):
         code = m * members + i
         found = jnp.int32(0)
         for a in range(members):
@@ -163,15 +173,18 @@
                 found = found + jnp.where(code == a * members + b, orders[a][b], 0)
         return found
 
-    def pass_on(s, next_place, goes_on):
-        to_chain(s, next_place).wait_recv()
+    orders = visiting_orders(members)
+    crossing, onward_order = return_orders(members)
+
+    def pass_on(s, h, next_place, goes_on):
+        to_chain(s, h, next_place).wait_recv()
 
         @pl.when(goes_on)
         def _():
-            to_chain(s, next_place).start()
-
-        to_x(s).start()
-        to_core(s).start()
+            to_chain(s, h, next_place).start()
+
+        to_x(s, h).start()
+        to_core(s, h).start()
 
     def core_copy(s):
         return pltpu.make_async_remote_copy(
@@ -183,46 +196,69 @@
             device_id_type=pl.DeviceIdType.MESH,
         )
 
-    def x_copy(s):
+    def piece(h):
+        return pl.ds(h * piece_rows, piece_rows)
+
+    def x_copy(s, h):
         return pltpu.make_async_remote_copy(
-            src_ref=core_sum.at[s, pl.ds(rows, rows), :],
-            dst_ref=x_in.at[s],
-            send_sem=x_send.at[s],
-            recv_sem=x_recv.at[s],
+            src_ref=core_sum.at[s, piece(h), :],
+            dst_ref=x_in.at[s, piece(h), :],
+            send_sem=x_send.at[s, h],
+            recv_sem=x_recv.at[s, h],
             device_id=x_peer,
             device_id_type=pl.DeviceIdType.MESH,
         )
 
-    def chain_copy(s, side, place):
+    def chain_copy(s, h, side, place):
         return pltpu.make_async_remote_copy(
-            src_ref=chain_out.at[s],
-            dst_ref=chain_in.at[side, s],
-            send_sem=chain_send.at[s],
-            recv_sem=chain_recv.at[side, s],
+            src_ref=chain_out.at[s, piece(h), :],
+            dst_ref=chain_in.at[side, s, piece(h), :],
+            send_sem=chain_send.at[s, h],
+            recv_sem=chain_recv.at[side, s, h],
             device_id=chain_peer(place),
             device_id_type=pl.DeviceIdType.MESH,
         )
 
     all_lane = lax.broadcasted_iota(jnp.int32, (4 * rows, block), 1) - off
     mine = (all_lane == me) | (all_lane == me + experts) | (all_lane == me + 2 * experts)
+
+    def add(a, b):
+        return a.astype(jnp.float32) + b.astype(jnp.float32)
+
+    def core_step(i):
+        s = looked_up(crossing, i)
+        core_copy(s).wait_recv()
+        for h in range(PIECES):
+            far = pl.ds(rows + h * piece_rows, piece_rows)
+            far_sum = add(partials[s, far, :], core_in[s, far, :])
+            core_sum[s, piece(h), :] = far_sum.astype(jnp.bfloat16)
+            x_copy(s, h).start()
 
     def gather_step(i, carry):
         left = m - i - 1
         right = m + i + 1
-
-        @pl.when(left >= 0)
-        def _():
-            pass_on(left, m + 1, has_right)
-
-        @pl.when(right < members)
-        def _():
-            pass_on(right, m - 1, has_left)
-
-        s = place_at(i)
-        to_x(s).wait_recv()
-        to_core_far(s).start()
-        to_core(s).wait_recv()
-        to_core_far(s).wait_recv()
+        for h in range(PIECES):
+
+            @pl.when(left >= 0)
+            def _():
+                pass_on(left, h, m + 1, has_right)
+
+            @pl.when(right < members)
+            def _():
+                pass_on(right, h, m - 1, has_left)
+
+        s = looked_up(orders, i)
+        for h in range(PIECES):
+            to_x(s, h).wait_recv()
+            to_core_far(s, h).start()
+
+        @pl.when(i == members - 1)
+        def _():
+            core_step(0)
+
+        for h in range(PIECES):
+            to_core(s, h).wait_recv()
+            to_core_far(s, h).wait_recv()
 
         @pl.when(i == 0)
         def _():
@@ -245,100 +281,103 @@
 
     lax.fori_loop(0, members, gather_step, 0)
 
-    def add(a, b):
-        return a.astype(jnp.float32) + b.astype(jnp.float32)
-
-    def core_step(i, carry):
-        s = place_at(members - 1 - i)
-        core_copy(s).wait_recv()
-        far = pl.ds(rows, rows)
-        core_sum[s, far, :] = add(partials[s, far, :], core_in[s, far, :]).astype(jnp.bfloat16)
-        x_copy(s).start()
+    def later_core_step(i, carry):
+        core_step(i)
         return carry
 
-    lax.fori_loop(0, members, core_step, 0)
-
-    def own_sum(s):
-        x_copy(s).wait_recv()
-        return add(partials[s, own_rows, :], core_in[s, own_rows, :]) + x_in[s].astype(jnp.float32)
+    lax.fori_loop(1, members, later_core_step, 0)
+
+    def own_sum(s, h):
+        x_copy(s, h).wait_recv()
+        near = add(partials[s, piece(h), :], core_in[s, piece(h), :])
+        return near + x_in[s, piece(h), :].astype(jnp.float32)
 
     def chain_step(i, carry):
-        s = place_at(members - 1 - i)
-        total = own_sum(s)
+        s = looked_up(onward_order, i)
 
         def onward(side, upstream, next_place):
-            @pl.when(upstream)
+            for h in range(PIECES):
+                total = own_sum(s, h)
+
+                @pl.when(upstream)
+                def _():
+                    chain_copy(s, h, side, next_place).wait_recv()
+                    arrived = chain_in[side, s, piece(h), :].astype(jnp.float32)
+                    chain_out[s, piece(h), :] = (total + arrived).astype(jnp.bfloat16)
+
+                @pl.when(jnp.logical_not(upstream))
+                def _():
+                    chain_out[s, piece(h), :] = total.astype(jnp.bfloat16)
+
+                chain_copy(s, h, side, next_place).start()
+
+        @pl.when(s > m)
+        def _():
+            onward(0, has_left, m + 1)
+
+        @pl.when(s < m)
+        def _():
+            onward(1, has_right, m - 1)
+
+        return carry
+
+    lax.fori_loop(0, members - 1, chain_step, 0)
+
+    for h in range(PIECES):
+        total = own_sum(m, h)
+
+        @pl.when(has_left & has_right)
+        def _():
+            chain_copy(m, h, 0, m + 1).wait_recv()
+            chain_copy(m, h, 1, m - 1).wait_recv()
+            both = add(chain_in[0, m, piece(h), :], chain_in[1, m, piece(h), :])
+            out_ref[piece(h), :] = (total + both).astype(out_ref.dtype)
+
+        @pl.when(has_left & jnp.logical_not(has_right))
+        def _():
+            chain_copy(m, h, 0, m - 1).wait_recv()
+            one = chain_in[0, m, piece(h), :].astype(jnp.float32)
+            out_ref[piece(h), :] = (total + one).astype(out_ref.dtype)
+
+        @pl.when(has_right & jnp.logical_not(has_left))
+        def _():
+            chain_copy(m, h, 1, m + 1).wait_recv()
+            one = chain_in[1, m, piece(h), :].astype(jnp.float32)
+            out_ref[piece(h), :] = (total + one).astype(out_ref.dtype)
+
+    for h in range(PIECES):
+
+        @pl.when(has_left)
+        def _():
+            to_left_first(h).wait_send()
+
+        @pl.when(has_right)
+        def _():
+            to_right_first(h).wait_send()
+
+    def finish(s, carry):
+        core_copy(s).wait_send()
+        for h in range(PIECES):
+            to_x(s, h).wait_send()
+            to_core(s, h).wait_send()
+            to_core_far(s, h).wait_send()
+            x_copy(s, h).wait_send()
+
+            @pl.when((s < m) & has_right)
             def _():
-                chain_copy(s, side, next_place).wait_recv()
-                chain_out[s] = (total + chain_in[side, s].astype(jnp.float32)).astype(jnp.bfloat16)
-
-            @pl.when(jnp.logical_not(upstream))
+                to_chain(s, h, m + 1).wait_send()
+
+            @pl.when((s > m) & has_left)
             def _():
-                chain_out[s] = total.astype(jnp.bfloat16)
-
-            chain_copy(s, side, next_place).start()
-
-        @pl.when(s > m)
-        def _():
-            onward(0, has_left, m + 1)
-
-        @pl.when(s < m)
-        def _():
-            onward(1, has_right, m - 1)
-
-        return carry
-
-    lax.fori_loop(0, members - 1, chain_step, 0)
-
-    total = own_sum(m)
-
-    @pl.when(has_left & has_right)
-    def _():
-        chain_copy(m, 0, m + 1).wait_recv()
-        chain_copy(m, 1, m - 1).wait_recv()
-        both = add(chain_in[0, m], chain_in[1, m])
-        out_ref[...] = (total + both).astype(out_ref.dtype)
-
-    @pl.when(has_left & jnp.logical_not(has_right))
-    def _():
-        chain_copy(m, 0, m - 1).wait_recv()
-        out_ref[...] = (total + chain_in[0, m].astype(jnp.float32)).astype(out_ref.dtype)
-
-    @pl.when(has_right & jnp.logical_not(has_left))
-    def _():
-        chain_copy(m, 1, m + 1).wait_recv()
-        out_ref[...] = (total + chain_in[1, m].astype(jnp.float32)).astype(out_ref.dtype)
-
-    @pl.when(has_left)
-    def _():
-        to_left_first().wait_send()
-
-    @pl.when(has_right)
-    def _():
-        to_right_first().wait_send()
-
-    def finish(s, carry):
-        to_x(s).wait_send()
-        to_core(s).wait_send()
-        to_core_far(s).wait_send()
-        core_copy(s).wait_send()
-        x_copy(s).wait_send()
-
-        @pl.when((s < m) & has_right)
-        def _():
-            to_chain(s, m + 1).wait_send()
-
-        @pl.when((s > m) & has_left)
-        def _():
-            to_chain(s, m - 1).wait_send()
-
-        @pl.when(s > m)
-        def _():
-            chain_copy(s, 0, m + 1).wait_send()
-
-        @pl.when(s < m)
-        def _():
-            chain_copy(s, 1, m - 1).wait_send()
+                to_chain(s, h, m - 1).wait_send()
+
+            @pl.when(s > m)
+            def _():
+                chain_copy(s, h, 0, m + 1).wait_send()
+
+            @pl.when(s < m)
+            def _():
+                chain_copy(s, h, 1, m - 1).wait_send()
 
         return carry
 
@@ -366,20 +405,20 @@
             pltpu.VMEM((hidden_width, width), jnp.bfloat16),
             pltpu.VMEM((members, 4 * rows, width), jnp.bfloat16),
             pltpu.VMEM((members, 2 * rows, width), jnp.bfloat16),
-            pltpu.VMEM((members, 2 * rows, width), jnp.bfloat16),
+            pltpu.VMEM((members, rows, width), jnp.bfloat16),
             pltpu.VMEM((members, rows, width), jnp.bfloat16),
             pltpu.VMEM((members, rows, width), jnp.bfloat16),
             pltpu.VMEM((2, members, rows, width), jnp.bfloat16),
             dma((2,)),
-            dma((4, members)),
-            dma((4, members)),
-            dma((2,)),
+            dma((4, members, PIECES)),
+            dma((4, members, PIECES)),
+            dma((2, PIECES)),
             dma((members,)),
             dma((members,)),
-            dma((members,)),
-            dma((members,)),
-            dma((members,)),
-            dma((2, members)),
+            dma((members, PIECES)),
+            dma((members, PIECES)),
+            dma((members, PIECES)),
+            dma((2, members, PIECES)),
         ],
         compiler_params=pltpu.CompilerParams(
             collective_id=0, has_side_effects=True, vmem_limit_bytes=60 * 2**20

time: 56.6 us -> 49.6 us (0.88)
  Pallas kernels: 54.8 us -> 47.8 us
    pallas_call x1, Pallas kernels: 54.8 us -> 47.8 us  [fused_on_device(): pl.pallas_call(functools.partial(fused_kernel, members), out_shape=jax.Sh...]
where the time goes in v3:
time: 49.6 us; the launch traced here: 49.5 us
  Pallas kernels  47.8 us (96%)
  local copies, waits for them, and re-layouts  1.61 us (3%)
    pallas_call x1, Pallas kernels, fused_on_device(): pl.pallas_call(functools.partial(fused_kernel, members), out_shape=jax.Sh...  47.8 us
    unnamed x1, local copies, waits for them, and re-layouts  1.61 us

profile of v3, /device:TPU:0, one launch (start us, length us, event | category | flops | bytes accessed | tf_op | source)
XLA Modules:
  0.0 49.5 jit_solution(1664743950111810758)
XLA Ops:
  0.0 47.8 %shard_map.64 = bf16[64,1344]{1,0:T(8,128)(2,1)} custom-call(bf16[64,1344]{1,0:T(8,128)(2,1)} %tok_ref.1, f32[1344]{0:T(1024)} %gain_ref.1, s32[6,64]{1,0:T(8,128)} %bitcast.4, f32[6,64]{1,0:T(8,128)} %bitcast.5, bf16[1,928,1344]{2,1,0:T(8,128)(2,1)} %bitcast.3, bf16[1,928,1344]{2,1,0:T(8,128)(2,1)} %down_hbm.1), custom_call_target="tpu_custom_call" | custom-call | flops 5108662272 | bytes 4988928 | tf_op jit(solution)/shard_map/pallas_call | solution.py:397
  47.9 1.6 %copy.8 = bf16[64,1344]{1,0:T(8,128)(2,1)} copy(bf16[64,1344]{1,0:T(8,128)(2,1)} %shard_map.64) | data formatting | bytes 344064

commit v4 on v3

--- a/solution.py
+++ b/solution.py
@@ -186,12 +186,12 @@
         to_x(s, h).start()
         to_core(s, h).start()
 
-    def core_copy(s):
+    def core_copy(s, line):
         return pltpu.make_async_remote_copy(
-            src_ref=partials.at[s, pl.ds(2 * rows, 2 * rows), :],
-            dst_ref=core_in.at[s],
-            send_sem=core_send.at[s],
-            recv_sem=core_recv.at[s],
+            src_ref=partials.at[s, pl.ds((2 + line) * rows, rows), :],
+            dst_ref=core_in.at[s, pl.ds(line * rows, rows), :],
+            send_sem=core_send.at[s, line],
+            recv_sem=core_recv.at[s, line],
             device_id=core_peer,
             device_id_type=pl.DeviceIdType.MESH,
         )
@@ -227,7 +227,7 @@
 
     def core_step(i):
         s = looked_up(crossing, i)
-        core_copy(s).wait_recv()
+        core_copy(s, 1).wait_recv()
         for h in range(PIECES):
             far = pl.ds(rows + h * piece_rows, piece_rows)
             far_sum = add(partials[s, far, :], core_in[s, far, :])
@@ -248,13 +248,13 @@
                 pass_on(right, h, m - 1, has_left)
 
         s = looked_up(orders, i)
+        @pl.when(i == members - 1)
+        def _():
+            core_step(0)
+
         for h in range(PIECES):
             to_x(s, h).wait_recv()
             to_core_far(s, h).start()
-
-        @pl.when(i == members - 1)
-        def _():
-            core_step(0)
 
         for h in range(PIECES):
             to_core(s, h).wait_recv()
@@ -276,7 +276,8 @@
         hidden = jnp.square(jnp.maximum(up_values, 0.0)).astype(jnp.bfloat16)
         down_values = jnp.dot(hidden, down_ref[...], preferred_element_type=jnp.float32)
         partials[s] = (down_values * row_weight).astype(jnp.bfloat16)
-        core_copy(s).start()
+        core_copy(s, 1).start()
+        core_copy(s, 0).start()
         return carry
 
     lax.fori_loop(0, members, gather_step, 0)
@@ -294,6 +295,7 @@
 
     def chain_step(i, carry):
         s = looked_up(onward_order, i)
+        core_copy(s, 0).wait_recv()
 
         def onward(side, upstream, next_place):
             for h in range(PIECES):
@@ -322,6 +324,7 @@
         return carry
 
     lax.fori_loop(0, members - 1, chain_step, 0)
+    core_copy(m, 0).wait_recv()
 
     for h in range(PIECES):
         total = own_sum(m, h)
@@ -356,7 +359,8 @@
             to_right_first(h).wait_send()
 
     def finish(s, carry):
-        core_copy(s).wait_send()
+        core_copy(s, 0).wait_send()
+        core_copy(s, 1).wait_send()
         for h in range(PIECES):
             to_x(s, h).wait_send()
             to_core(s, h).wait_send()
@@ -413,8 +417,8 @@
             dma((4, members, PIECES)),
             dma((4, members, PIECES)),
             dma((2, PIECES)),
-            dma((members,)),
-            dma((members,)),
+            dma((members, 2)),
+            dma((members, 2)),
             dma((members, PIECES)),
             dma((members, PIECES)),
             dma((members, PIECES)),
@@ -509,7 +513,7 @@
         P(("parts", "group", "member"), None),
     )
     out_specs = P(("parts", "group", "member"), "half")
-    fused = mesh.shape["half"] == 1 and mesh.shape["group"] == 4 and 1 < mesh.shape["member"] <= 4
+    fused = mesh.shape["half"] == 1 and mesh.shape["group"] == 4 and mesh.shape["member"] == 4
     on_device = fused_on_device if fused else routed_on_device
     return jax.shard_map(
         on_device, mesh=mesh, in_specs=in_specs, out_specs=out_specs, check_vma=False

time: 49.6 us -> 49.4 us (level)
  no operation moved by 1% of the time
where the time goes in v4:
time: 49.4 us; the launch traced here: 49.3 us
  Pallas kernels  47.7 us (97%)
  local copies, waits for them, and re-layouts  1.61 us (3%)
    pallas_call x1, Pallas kernels, fused_on_device(): pl.pallas_call(functools.partial(fused_kernel, members), out_shape=jax.Sh...  47.7 us
    unnamed x1, local copies, waits for them, and re-layouts  1.61 us

profile of v4, /device:TPU:0, one launch (start us, length us, event | category | flops | bytes accessed | tf_op | source)
XLA Modules:
  0.0 49.3 jit_solution(15490757399733907600)
XLA Ops:
  0.0 47.7 %shard_map.64 = bf16[64,1344]{1,0:T(8,128)(2,1)} custom-call(bf16[64,1344]{1,0:T(8,128)(2,1)} %tok_ref.1, f32[1344]{0:T(1024)} %gain_ref.1, s32[6,64]{1,0:T(8,128)} %bitcast.4, f32[6,64]{1,0:T(8,128)} %bitcast.5, bf16[1,928,1344]{2,1,0:T(8,128)(2,1)} %bitcast.3, bf16[1,928,1344]{2,1,0:T(8,128)(2,1)} %down_hbm.1), custom_call_target="tpu_custom_call" | custom-call | flops 5108662272 | bytes 4988928 | tf_op jit(solution)/shard_map/pallas_call | solution.py:401
  47.7 1.6 %copy.8 = bf16[64,1344]{1,0:T(8,128)(2,1)} copy(bf16[64,1344]{1,0:T(8,128)(2,1)} %shard_map.64) | data formatting | bytes 344064
